TPU v7x, 512 devices: a whole 4x4x16 slice. The times are simulated.
512 devices in a mesh: ctx: 64 (over y, z), head: 8 (over x, core).
Axes of the slice: x: 4, y: 4, z: 16, core: 2. Of those that a mesh axis runs over, the one named last changes fastest.
Arguments:
- queries: bfloat16 [16384, 4096], P('ctx', 'head'), may hold values from -200 to 200
- span_keys: bfloat16 [16384, 4096], P('ctx', 'head'), may hold values from -6 to 6
- span_values: bfloat16 [16384, 4096], P('ctx', 'head'), may hold values from -96 to 96
- cache_keys: bfloat16 [65536, 4096], P('ctx', 'head'), may hold values from -6 to 6
- cache_values: bfloat16 [65536, 4096], P('ctx', 'head'), may hold values from -96 to 96
- land_keys: bfloat16 [1024, 4096], P('ctx', 'head'), may hold values from -4.5 to 4.5
- land_values: bfloat16 [1024, 4096], P('ctx', 'head'), may hold values from -96 to 96
- out_weight: bfloat16 [4096, 4096], P('head', 'ctx'), may hold values from -0.09375 to 0.09375
- selection: int32 [256, 32, 4], P('ctx', 'head'), may hold values from 0 to 1023, as said below
Outputs:
- projected: bfloat16 [16384, 4096], P('ctx', 'head')
Inputs may be any that keep to these rules, and one draw needn't show every extreme that they name: `selection`: the 4 blocks of one query group and head are distinct. Count block b as owned by ctx index b // 16. Over all groups and heads of one device (one index of ctx and one of head), the selections within one owner's blocks number at most 4 and form at most 1 distinct pairs of block and head; some owner receives exactly that many of both from every device.
All inputs are finite; a program needn't handle non-finite values.
Results may differ from a plain program's by a relative error of at most 0.015.
Values may be sent and summed in bfloat16 or wider, within the bound.
A program may use at most 64 MiB of HBM per device.

v0:
```python
import math

import jax
import jax.numpy as jnp
from jax import lax
from jax.sharding import Mesh
from jax.sharding import PartitionSpec as P

BLOCK = 64
CTX = ("ctx_0", "ctx_1")


def in_one_piece(arrays, axis, dim, along):
    ends, at = ([], 0)
    for a in arrays[:-1]:
        at += a.shape[along]
        ends.append(at)
    both = jnp.concatenate(arrays, axis=along)
    return tuple(jnp.split(lax.all_gather(both, axis, axis=dim, tiled=True), ends, axis=along))


def cut_along(array, dim, peers):
    before, after = (array.shape[:dim], array.shape[dim + 1 :])
    return jnp.moveaxis(array.reshape(*before, peers, -1, *after), dim, 0)


def joined_along(tiles, dim):
    shape = list(tiles.shape[1:])
    shape[dim] *= tiles.shape[0]
    return jnp.moveaxis(tiles, 0, dim).reshape(shape)


def turned_blocks(tiles, axes, turns):
    shape = [lax.axis_size(a) for a in axes]
    tiles = tiles.reshape(*shape, *tiles.shape[1:])
    for k in turns:
        tiles = lax.all_to_all(tiles, axes[k], split_axis=k, concat_axis=k, tiled=True)
    return tiles.reshape(-1, *tiles.shape[len(axes) :])


def stepwise_exchange(array, axes, turns, split_dim, concat_dim):
    tiles = cut_along(array, split_dim, lax.axis_size(axes))
    return joined_along(turned_blocks(tiles, axes, turns), concat_dim)


def gather_in_order(array, axes, turns):
    tiles = array[None]
    for k in turns:
        tiles = lax.all_gather(tiles, axes[k], axis=0, tiled=True)
    current = [lax.axis_size(axes[k]) for k in reversed(turns)]
    tiles = tiles.reshape(*current, *array.shape)
    turned = sorted(range(len(turns)), key=lambda place: turns[len(turns) - 1 - place])
    return tiles.transpose(*turned, *range(len(turns), tiles.ndim)).reshape(-1, *array.shape)


def gathered_by_axis(array, axes, turns, dim):
    return joined_along(gather_in_order(array, axes, turns), dim)


def sum_at_owner(array, axis, dim):
    peers = lax.axis_size(axis)
    tiles = lax.all_to_all(cut_along(array, dim, peers), axis, 0, 0, tiled=True)
    return jnp.sum(tiles.astype(jnp.float32), axis=0)


def local(
    queries,
    span_keys,
    span_values,
    cache_keys,
    cache_values,
    land_keys,
    land_values,
    out_weight,
    selection,
):
    query_rows, row_width = queries.shape
    groups, head_dev, pick_count = selection.shape
    head_size = row_width // head_dev
    blocks_dev = cache_keys.shape[0] // BLOCK
    devices = lax.axis_size(CTX)
    scaling = 1.0 / math.sqrt(head_size)
    query_heads = queries.reshape(query_rows, head_dev, head_size)
    pieces = in_one_piece((land_keys, land_values), CTX, 0, 1)
    run_max = jnp.full((head_dev, query_rows), -jnp.inf, jnp.float32)
    run_sum = jnp.zeros((head_dev, query_rows), jnp.float32)
    run_acc = jnp.zeros((head_dev, query_rows, head_size), jnp.float32)
    key_piece = pieces[0].reshape(-1, head_dev, head_size)
    value_piece = pieces[1].reshape(-1, head_dev, head_size)
    scores = (
        jnp.einsum("qhd,nhd->hqn", query_heads, key_piece, preferred_element_type=jnp.float32)
        * scaling
    )
    new_max = jnp.max(scores, axis=2)
    weights = jnp.exp(scores - new_max[:, :, None])
    factor = jnp.exp(run_max - new_max)
    new_sum = run_sum * factor + jnp.sum(weights, axis=2)
    new_acc = run_acc * factor[:, :, None] + jnp.einsum(
        "hqn,nhd->hqd",
        weights.astype(jnp.bfloat16),
        value_piece,
        preferred_element_type=jnp.float32,
    )
    request_count = groups * head_dev * pick_count
    owners_flat = (selection // blocks_dev).reshape(request_count)
    block_flat = (selection % blocks_dev).reshape(request_count)
    head_flat = jnp.broadcast_to(
        jnp.arange(head_dev, dtype=jnp.int32)[None, :, None], selection.shape
    ).reshape(request_count)
    request_order = jnp.arange(request_count)
    earlier = request_order[None, :] < request_order[:, None]
    same_owner = owners_flat[:, None] == owners_flat[None, :]
    distinct_most = (head_dev * 2 * pick_count + devices - 1) // devices
    key_blocks = cache_keys.reshape(blocks_dev, BLOCK, head_dev, head_size)
    value_blocks = cache_values.reshape(blocks_dev, BLOCK, head_dev, head_size)
    asked_pairs = jnp.stack([block_flat, head_flat], axis=1)
    pair_ids = selection.reshape(request_count) * head_dev + head_flat
    same_pair = pair_ids[:, None] == pair_ids[None, :]
    is_first = jnp.logical_not(jnp.any(same_pair & earlier, axis=1))
    first_rank = jnp.sum(same_owner & earlier & is_first[None, :], axis=1)
    slot_ids = jnp.sum(jnp.where(same_pair & is_first[None, :], first_rank[None, :], 0), axis=1)
    wanted = (
        jnp.zeros((devices, distinct_most, 2), jnp.int32).at[owners_flat, slot_ids].set(asked_pairs)
    )
    asked_for = stepwise_exchange(wanted, CTX, (0, 1), 0, 0)
    sent_keys = key_blocks[asked_for[:, :, 0], :, asked_for[:, :, 1], :]
    sent_values = value_blocks[asked_for[:, :, 0], :, asked_for[:, :, 1], :]
    fetched_keys = lax.all_to_all(sent_keys, CTX, split_axis=0, concat_axis=0, tiled=True)
    fetched_values = lax.all_to_all(sent_values, CTX, split_axis=0, concat_axis=0, tiled=True)
    owner_grid = owners_flat.reshape(selection.shape)
    slot_grid = slot_ids.reshape(selection.shape)
    chosen_keys = fetched_keys[owner_grid, slot_grid]
    chosen_values = fetched_values[owner_grid, slot_grid].reshape(
        groups, head_dev, pick_count * BLOCK, head_size
    )
    query_groups = query_heads.reshape(groups, BLOCK, head_dev, head_size)
    chosen_scores = (
        jnp.einsum(
            "gqhd,ghpkd->ghqpk", query_groups, chosen_keys, preferred_element_type=jnp.float32
        )
        * scaling
    )
    chosen_scores = chosen_scores.reshape(groups, head_dev, BLOCK, pick_count * BLOCK)
    local_keys = span_keys.reshape(groups, BLOCK, head_dev, head_size)
    local_values = span_values.reshape(groups, BLOCK, head_dev, head_size)
    causal = jnp.arange(BLOCK)[:, None] >= jnp.arange(BLOCK)[None, :]
    local_scores = (
        jnp.einsum("gqhd,gkhd->ghqk", query_groups, local_keys, preferred_element_type=jnp.float32)
        * scaling
    )
    local_scores = jnp.where(causal[None, None], local_scores, -jnp.inf)
    land_top = jnp.transpose(new_max.reshape(head_dev, groups, BLOCK), (1, 0, 2))
    land_total = jnp.transpose(new_sum.reshape(head_dev, groups, BLOCK), (1, 0, 2))
    land_part = jnp.transpose(new_acc.reshape(head_dev, groups, BLOCK, head_size), (1, 0, 2, 3))
    overall_top = jnp.maximum(
        jnp.maximum(land_top, jnp.max(chosen_scores, axis=3)), jnp.max(local_scores, axis=3)
    )
    land_weight = jnp.exp(land_top - overall_top)
    chosen_weights = jnp.exp(chosen_scores - overall_top[..., None])
    local_weights = jnp.exp(local_scores - overall_top[..., None])
    denominator = (
        land_total * land_weight + jnp.sum(chosen_weights, axis=3) + jnp.sum(local_weights, axis=3)
    )
    numerator = land_part * land_weight[..., None]
    numerator = numerator + jnp.einsum(
        "ghqn,ghnd->ghqd",
        chosen_weights.astype(jnp.bfloat16),
        chosen_values,
        preferred_element_type=jnp.float32,
    )
    numerator = numerator + jnp.einsum(
        "ghqk,gkhd->ghqd",
        local_weights.astype(jnp.bfloat16),
        local_values,
        preferred_element_type=jnp.float32,
    )
    attended = (numerator / denominator[..., None]).astype(jnp.bfloat16)
    attended = jnp.transpose(attended, (0, 2, 1, 3)).reshape(query_rows, row_width)
    partial_out = jnp.dot(
        attended, gathered_by_axis(out_weight, CTX, (0, 1), 1), preferred_element_type=jnp.float32
    )
    summed = sum_at_owner(partial_out.astype(jnp.bfloat16), "head", 1)
    return summed.astype(jnp.bfloat16)


def solution(mesh):
    torus = Mesh(mesh.devices.reshape(4, 16, mesh.shape["head"]), ("ctx_0", "ctx_1", "head"))
    in_specs = (
        P(CTX, "head"),
        P(CTX, "head"),
        P(CTX, "head"),
        P(CTX, "head"),
        P(CTX, "head"),
        P(CTX, "head"),
        P(CTX, "head"),
        P("head", CTX),
        P(CTX, "head", None),
    )
    out_specs = P(CTX, "head")
    return jax.shard_map(local, mesh=torus, in_specs=in_specs, out_specs=out_specs, check_vma=False)
```

profile of v0, /device:TPU:1, one launch (start us, length us, event | category | flops | bytes accessed | tf_op | source)
XLA Modules:
  0.0 299.0 jit_solution(17440961947433692486)
XLA Ops:
  6.5 1.3 pad_maximum_fusion
  7.9 0.7 add_select_fusion
  8.9 0.2 fusion.32
  9.1 0.1 stack_reshape.4
  9.3 0.1 copy.165
  9.4 0.2 convert_reduce_fusion
  9.6 0.2 select_reduce_fusion
  9.8 0.8 scatter_custom_fusion
  10.7 8.9 %all_to_all.25 = s32[4,16,1,1,2]{1,4,3,2,0:T(2,128)S(1)} all-to-all(s32[4,16,1,1,2]{1,4,3,2,0:T(2,128)S(1)} %copy.167), channel_id=1, replica_groups=mesh['ctx_0'=4,'ctx_1'=16,'head'=8] {'ctx_0'}, dimensions={0} | all-to-all | bytes 1024 | tf_op jit(solution)/shard_map/all_to_all | solution.py:37
  19.6 0.7 copy.168
  20.3 14.9 %all-to-all-start.1 = ((s32[4,16,1,1,2]{0,4,3,2,1:T(2,128)}), s32[4,16,1,1,2]{0,4,3,2,1:T(2,128)S(1)}, u32[]{:S(2)}, u32[]{:S(2)}) async-start(s32[4,16,1,1,2]{0,4,3,2,1:T(2,128)} %copy.168), calls=%async_computation.1 | async-start | bytes 32768 | tf_op jit(solution)/shard_map/all_to_all | solution.py:37
  35.2 1.4 reshape.202
  36.6 0.3 copy.170
  36.9 9.7 %all-to-all-done.1 = s32[4,16,1,1,2]{0,4,3,2,1:T(2,128)S(1)} async-done(((s32[4,16,1,1,2]{0,4,3,2,1:T(2,128)}), s32[4,16,1,1,2]{0,4,3,2,1:T(2,128)S(1)}, u32[]{:S(2)}, u32[]{:S(2)}) %all-to-all-start.1) | async-done | bytes 544 | tf_op jit(solution)/shard_map/all_to_all | solution.py:37
  46.8 1.7 gather_fusion
  48.6 4.7 %all-to-all-start.2 = ((bf16[64,1,64,128]{3,2,1,0:T(8,128)(2,1)}), bf16[64,1,64,128]{3,2,1,0:T(8,128)(2,1)S(1)}, u32[]{:S(2)}, u32[]{:S(2)}) async-start(bf16[64,1,64,128]{3,2,1,0:T(8,128)(2,1)} %bitcast.12), calls=%async_computation.2 | async-start | bytes 2097152 | tf_op jit(solution)/shard_map/all_to_all | solution.py:128
  53.3 10.7 %all-gather = bf16[2048,64]{0,1:T(8,128)(2,1)S(1)} all-gather(bf16[512,64]{0,1:T(8,128)(2,1)S(1)} %copy-done.5), channel_id=2, replica_groups=mesh['ctx_0'=4,'ctx_1'=16,'head'=8] {'ctx_0'}, dimensions={0}, use_global_device_ids=true | all-gather | bytes 327680 | tf_op jit(solution)/shard_map/all_gather | solution.py:49
  63.9 0.7 copy.237
  64.7 0.3 reshape.208
  65.0 0.3 copy.177
  65.3 1.8 gather_fusion.2
  67.1 35.5 %all-to-all-done.2 = bf16[64,1,64,128]{3,2,1,0:T(8,128)(2,1)S(1)} async-done(((bf16[64,1,64,128]{3,2,1,0:T(8,128)(2,1)}), bf16[64,1,64,128]{3,2,1,0:T(8,128)(2,1)S(1)}, u32[]{:S(2)}, u32[]{:S(2)}) %all-to-all-start.2) | async-done | bytes 1048608 | tf_op jit(solution)/shard_map/all_to_all | solution.py:128
  102.5 11.3 %all-to-all-start.3 = ((bf16[64,1,64,128]{3,2,1,0:T(8,128)(2,1)}), bf16[64,1,64,128]{3,2,1,0:T(8,128)(2,1)S(1)}, u32[]{:S(2)}, u32[]{:S(2)}) async-start(bf16[64,1,64,128]{3,2,1,0:T(8,128)(2,1)} %bitcast.22), calls=%async_computation.3 | async-start | bytes 2097152 | tf_op jit(solution)/shard_map/all_to_all | solution.py:129
  114.1 1.1 reshape.206
  115.3 1.7 reshape.210
  117.0 1.1 fusion.50
  118.1 55.5 %all-gather.4.cloned.1.call-done = bf16[1024,1024]{1,0:T(8,128)(2,1)} async-done(((bf16[16,1024]{1,0:T(8,128)(2,1)}), bf16[1024,1024]{1,0:T(8,128)(2,1)}) %all-gather.4.cloned.1.call-update) | async-done | bytes 2097168 | tf_op jit(solution)/shard_map/all_gather | solution.py:19
  173.6 2.7 fusion.49
  176.3 2.3 copy.196
  178.5 4.0 %bitcast_reduce_fusion = (f32[4,256]{1,0:T(4,128)S(1)}, f32[4,1024,256]{2,1,0:T(8,128)}) fusion(bf16[1024,4,128]{0,2,1:T(8,128)(2,1)} %bitcast.142, bf16[256,512]{1,0:T(8,128)(2,1)S(1)} %copy-done), kind=kOutput, calls=%fused_computation.7 | convolution fusion | flops 270531584 | bytes 5509120 | tf_op jit(solution)/shard_map/qhd,nhd->hqn/dot_general | solution.py:91
  182.6 2.9 fusion.1
  185.6 1.3 copy.197
  186.9 4.4 %fusion.11 = f32[4,256,128]{2,1,0:T(8,128)} fusion(bf16[1024,4,128]{0,2,1:T(8,128)(2,1)} %bitcast.141, f32[4,1024,256]{2,1,0:T(8,128)} %get-tuple-element.19, f32[4,256]{1,0:T(4,128)S(1)} %get-tuple-element.18, f32[4,256]{1,0:T(4,128)S(1)} %exponential_multiply_fusion), kind=kOutput, calls=%fused_computation.24 | convolution fusion | flops 271712256 | bytes 5775360 | tf_op jit(solution)/shard_map/hqn,nhd->hqd/dot_general | solution.py:98
  191.3 1.7 gather_fusion.1
  192.9 1.7 bitcast_reduce_fusion.1
  194.6 1.6 copy.176
  196.2 1.7 gather_fusion.3
  197.9 1.2 fusion.18
  199.1 0.4 fusion.6
  199.5 1.3 convolution_bitcast_fusion
  200.8 2.2 fusion.16
  203.1 0.2 copy.183
  203.3 44.0 %all-gather.6.cloned.1.call-done = bf16[64,512,64]{1,2,0:T(8,128)(2,1)} async-done(((bf16[4,512,64]{1,2,0:T(8,128)(2,1)}), bf16[64,512,64]{1,2,0:T(8,128)(2,1)}) %all-gather.6.cloned.1.call-update) | async-done | bytes 4194320 | tf_op jit(solution)/shard_map/all_gather | solution.py:49
  247.3 2.7 copy.185
  250.0 1.3 convolution_convert_fusion
  251.3 0.2 copy.236
  251.4 39.7 %all_to_all.26 = bf16[8,256,512]{2,1,0:T(8,128)(2,1)S(1)} all-to-all(bf16[8,256,512]{2,1,0:T(8,128)(2,1)S(1)} %bitcast.138), channel_id=1, replica_groups=mesh['ctx_0'=4,'ctx_1'=16,'head'=8] {'head'}, dimensions={0} | all-to-all | bytes 4194304 | tf_op jit(solution)/shard_map/all_to_all | solution.py:62
  291.1 1.0 reduce_sum.74
  (41 shorter events, 1.3 us)
Async XLA Ops:
  6.5 167.1 %all-gather.4.cloned.1.call-start = ((), (), s32[]{:S(2)}) async-start(), calls=%async_computation.5 | async-start | bytes 2129920 | tf_op jit(solution)/shard_map/all_gather | solution.py:19
  20.3 26.3 %all-to-all-start.1 = ((s32[4,16,1,1,2]{0,4,3,2,1:T(2,128)}), s32[4,16,1,1,2]{0,4,3,2,1:T(2,128)S(1)}, u32[]{:S(2)}, u32[]{:S(2)}) async-start(s32[4,16,1,1,2]{0,4,3,2,1:T(2,128)} %copy.168), calls=%async_computation.1 | async-start | bytes 32768 | tf_op jit(solution)/shard_map/all_to_all | solution.py:37
  35.2 18.1 %copy-start.5 = (bf16[512,64]{0,1:T(8,128)(2,1)S(1)}, bf16[512,64]{0,1:T(8,128)(2,1)}, u32[]{:S(2)}) copy-start(bf16[512,64]{0,1:T(8,128)(2,1)} %param.16) | copy-start | bytes 196612
  36.9 27.8 %copy-start.2 = (bf16[1024,512]{1,0:T(8,128)(2,1)S(1)}, bf16[1024,512]{1,0:T(8,128)(2,1)}, u32[]{:S(2)}) copy-start(bf16[1024,512]{1,0:T(8,128)(2,1)} %param.13) | copy-start | bytes 3145732
  48.6 54.0 %all-to-all-start.2 = ((bf16[64,1,64,128]{3,2,1,0:T(8,128)(2,1)}), bf16[64,1,64,128]{3,2,1,0:T(8,128)(2,1)S(1)}, u32[]{:S(2)}, u32[]{:S(2)}) async-start(bf16[64,1,64,128]{3,2,1,0:T(8,128)(2,1)} %bitcast.12), calls=%async_computation.2 | async-start | bytes 2097152 | tf_op jit(solution)/shard_map/all_to_all | solution.py:128
  53.2 194.1 %all-gather.6.cloned.1.call-start = ((), (), s32[]{:S(2)}) async-start(), calls=%async_computation.6 | async-start | bytes 4456448 | tf_op jit(solution)/shard_map/all_gather | solution.py:49
  64.7 49.4 %copy-start = (bf16[256,512]{1,0:T(8,128)(2,1)S(1)}, bf16[256,512]{1,0:T(8,128)(2,1)}, u32[]{:S(2)}) copy-start(bf16[256,512]{1,0:T(8,128)(2,1)} %param.9) | copy-start | bytes 786436
  102.5 93.7 %all-to-all-start.3 = ((bf16[64,1,64,128]{3,2,1,0:T(8,128)(2,1)}), bf16[64,1,64,128]{3,2,1,0:T(8,128)(2,1)S(1)}, u32[]{:S(2)}, u32[]{:S(2)}) async-start(bf16[64,1,64,128]{3,2,1,0:T(8,128)(2,1)} %bitcast.22), calls=%async_computation.3 | async-start | bytes 2097152 | tf_op jit(solution)/shard_map/all_to_all | solution.py:129
  114.1 4.0 %copy-start.3 = (bf16[4,64,4,128]{3,2,1,0:T(4,128)(2,1)}, bf16[4,64,4,128]{3,2,1,0:T(4,128)(2,1)S(1)}, u32[]{:S(2)}) copy-start(bf16[4,64,4,128]{3,2,1,0:T(4,128)(2,1)S(1)} %reshape_reshape.11) | copy-start | bytes 786436
  186.9 6.1 %copy-start.4 = (bf16[4,64,4,128]{3,2,1,0:T(4,128)(2,1)S(1)}, bf16[4,64,4,128]{3,2,1,0:T(4,128)(2,1)}, u32[]{:S(2)}) copy-start(bf16[4,64,4,128]{3,2,1,0:T(4,128)(2,1)} %copy-done.3) | copy-start | bytes 786436
  194.6 4.8 %copy-start.1 = (bf16[4,64,4,128]{3,2,1,0:T(4,128)(2,1)S(1)}, bf16[4,64,4,128]{3,2,1,0:T(4,128)(2,1)}, u32[]{:S(2)}) copy-start(bf16[4,64,4,128]{3,2,1,0:T(4,128)(2,1)} %reshape.210) | copy-start | bytes 786436
Sparse Core Ops, SparseCore 0:
  10.3 163.2 all-gather.3
  175.7 71.5 all-gather.5
where the time goes:
time: 300 us; the launch traced here: 299 us
  waiting for transfers between devices  145 us (48%)
  blocking collectives  59.3 us (20%)
  starting transfers between devices  30.9 us (10%)
  local copies, waits for them, and re-layouts  26.3 us (9%)
  matrix products  16 us (5%)
  between operations  13.7 us (5%)
  other arithmetic  8.17 us (3%)
    all_gather x1, waiting for transfers between devices, in_one_piece(): lax.all_gather(both, axis, axis=dim, tiled=True)  55.5 us
    all_gather x1, waiting for transfers between devices, gather_in_order(): tiles = lax.all_gather(tiles, axes[k], axis=0, tiled=True)  44 us
    all_to_all x1, blocking collectives, sum_at_owner(): tiles = lax.all_to_all(cut_along(array, dim, peers), axis, 0, 0, tiled=True)  39.7 us
    all_to_all x1, waiting for transfers between devices, local(): lax.all_to_all(sent_keys, CTX, split_axis=0, concat_axis=0, tiled=True)  35.5 us
    all_to_all x1, starting transfers between devices, turned_blocks(): lax.all_to_all(tiles, axes[k], split_axis=k, concat_axis=k, tiled=True)  14.9 us
    all_to_all x1, starting transfers between devices, local(): lax.all_to_all(sent_values, CTX, split_axis=0, concat_axis=0, tiled=True)  11.3 us
    all_gather x1, blocking collectives, gather_in_order(): tiles = lax.all_gather(tiles, axes[k], axis=0, tiled=True)  10.7 us
    all_to_all x1, waiting for transfers between devices, turned_blocks(): lax.all_to_all(tiles, axes[k], split_axis=k, concat_axis=k, tiled=True)  9.71 us
  transfers between devices with their start and end apart: 5, of which 4 were waited for; matrix products, arithmetic and copies ran while one was open for 15% of the time, Pallas kernels for 0%

commit v1 on v0

v1 whole, which is shorter than its diff:
```python
import functools
import math

import jax
import jax.numpy as jnp
from jax import lax
from jax.experimental import pallas as pl
from jax.experimental.pallas import tpu as pltpu
from jax.sharding import PartitionSpec as P

MESH = pl.DeviceIdType.MESH
BLOCK = 64
NY, NZ, NX = 4, 16, 4
NCTX = NY * NZ
GROUPS, HEADS, PICKS, DH = 4, 4, 4, 128
ROWS, WIDTH = GROUPS * BLOCK, HEADS * DH
LAND = 16
BLOCKS = 16
STEPS = NZ // 2
NT = (((1,), (1,)), ((), ()))
SCALE = 1.0 / math.sqrt(DH)


def offsets(i):
    k, dy = lax.div(i, 4), lax.rem(i, 4)
    odd = lax.rem(k, 2)
    dz = lax.rem(odd * lax.div(k + 1, 2) + (1 - odd) * (NZ - lax.div(k, 2)), NZ)
    return dy, dz


def slot_of(dy, dz):
    k = jnp.where(dz == 0, 0, jnp.where(dz <= 8, 2 * dz - 1, 2 * (NZ - dz)))
    return 4 * k + dy


def slots_of(picks):
    ctx = lax.axis_index("ctx")
    owner = picks >> 4
    return slot_of(((ctx >> 4) - (owner >> 4)) & 3, ((ctx & 15) - (owner & 15)) & 15)


def remote(src, dst, send, recv, ctx, head):
    return pltpu.make_async_remote_copy(
        src_ref=src,
        dst_ref=dst,
        send_sem=send,
        recv_sem=recv,
        device_id=(ctx, head),
        device_id_type=MESH,
    )


def kernel(
    slots,
    pick_row,
    q,
    sk,
    sv,
    ck,
    cv,
    land,
    wt,
    out,
    pick_all,
    code_v,
    code_s,
    land_all,
    w_lane,
    w_all,
    send_k,
    send_v,
    recv_k,
    recv_v,
    att,
    prob,
    acc,
    top,
    tot,
    sums,
    pair_k,
    pair_v,
    pick_sem,
    code_sem,
    land_s,
    land_r,
    swap_sem,
    wz_s,
    wz_r,
    core_sem,
    yl_s,
    yl_r,
    yw_s,
    yw_r,
    kv_s,
    kv_r,
    mate_s,
    mate_r,
    xs_s,
    xs_r,
    fwd_s,
    fwd_r,
    far_s,
    far_r,
    ffw_s,
    ffw_r,
):
    ctx, head = lax.axis_index("ctx"), lax.axis_index("head")
    y, z = lax.div(ctx, NZ), lax.rem(ctx, NZ)
    x, core = lax.div(head, 2), lax.rem(head, 2)
    mate = 2 * x + 1 - core
    x_up, x_dn = lax.rem(x + 1, NX), lax.rem(x + NX - 1, NX)
    x_far = lax.rem(x + 2, NX)
    y_up, y_dn = lax.rem(y + 1, NY), lax.rem(y + NY - 1, NY)
    y_far = lax.rem(y + 2, NY)
    z_up = y * NZ + lax.rem(z + 1, NZ)
    z_dn = y * NZ + lax.rem(z + NZ - 1, NZ)
    swap_ctx, swap_head = x * NZ + z, 2 * y + core
    off_diag = x != y

    def peer(i):
        dy, dz = offsets(i)
        return lax.rem(y + dy, NY) * NZ + lax.rem(z + dz, NZ)

    barrier = pltpu.get_barrier_semaphore()

    def greet(i, carry):
        pl.semaphore_signal(
            barrier, inc=1, device_id=(peer(i), head), device_id_type=MESH
        )
        return carry

    lax.fori_loop(1, NCTX, greet, 0)
    for h in (mate, 2 * x_up + core, 2 * x_dn + core):
        pl.semaphore_signal(barrier, inc=1, device_id=(ctx, h), device_id_type=MESH)

    @pl.when(off_diag)
    def _():
        pl.semaphore_signal(
            barrier, inc=1, device_id=(swap_ctx, swap_head), device_id_type=MESH
        )

    land_all[ctx] = land[...]

    @pl.when(x == y)
    def _():
        w_lane[z] = wt[...]

    def split(b, carry):
        rows = pl.ds(pl.multiple_of(b * BLOCK, BLOCK), BLOCK)
        for h in range(HEADS):
            pair_k[b * HEADS + h] = ck[rows, h * DH : (h + 1) * DH]
            pair_v[b * HEADS + h] = cv[rows, h * DH : (h + 1) * DH]
        return carry

    lax.fori_loop(0, BLOCKS, split, 0)

    pl.semaphore_wait(barrier, NCTX - 1 + 3 + jnp.where(off_diag, 1, 0))

    def ring(buf, base, s, d, send, recv):
        slot = base + lax.rem(z + (NZ - s if d == 0 else s), NZ)
        return remote(
            buf.at[slot],
            buf.at[slot],
            send.at[d, s],
            recv.at[d, s],
            z_up if d == 0 else z_dn,
            head,
        )

    def ring_in(buf, base, s, d, send, recv):
        slot = base + lax.rem(z + (NZ - s - 1 if d == 0 else s + 1), NZ)
        return remote(
            buf.at[slot],
            buf.at[slot],
            send.at[d, s],
            recv.at[d, s],
            z_up if d == 0 else z_dn,
            head,
        )

    land_ring = functools.partial(ring, land_all, y * NZ)
    land_in = functools.partial(ring_in, land_all, y * NZ)
    w_ring = functools.partial(ring, w_lane, 0)
    w_in = functools.partial(ring_in, w_lane, 0)
    for d in (0, 1):
        land_ring(0, d, land_s, land_r).start()
    swap = remote(
        wt, w_lane.at[z], swap_sem.at[0], swap_sem.at[1], swap_ctx, swap_head
    )

    @pl.when(off_diag)
    def _():
        swap.start()

    own_picks = pltpu.make_async_copy(pick_row, pick_all.at[ctx], pick_sem.at[1])
    own_picks.start()

    def tell(i, carry):
        remote(
            pick_row,
            pick_all.at[ctx],
            pick_sem.at[0],
            pick_sem.at[1],
            peer(i),
            head,
        ).start()
        return carry

    lax.fori_loop(1, NCTX, tell, 0)

    @pl.when(off_diag)
    def _():
        swap.wait_recv()

    for d in (0, 1):
        w_ring(0, d, wz_s, wz_r).start()
    pltpu.make_async_copy(pick_all, pick_all, pick_sem.at[1]).wait()
    asked = pick_all[:, 0, :]
    lane = lax.broadcasted_iota(jnp.int32, asked.shape, 1)
    mine = jnp.logical_and(lane < GROUPS * HEADS * PICKS, (asked >> 4) == ctx)
    code = jnp.where(mine, (asked & 15) * HEADS + ((lane >> 2) & 3), 0)
    code = jnp.max(code, axis=1, keepdims=True)
    code_v[...] = jnp.broadcast_to(code, code_v.shape)
    to_scalar = pltpu.make_async_copy(code_v, code_s, code_sem.at[0])
    to_scalar.start()
    to_scalar.wait()

    def block_for(cache, t):
        return cache[code_s[t, 0]]

    recv_k[0] = block_for(pair_k, ctx)
    recv_v[0] = block_for(pair_v, ctx)

    def send_block(cache, out_buf, in_buf, which, i, carry):
        t = peer(i)
        out_buf[i] = block_for(cache, t)
        remote(
            out_buf.at[i], in_buf.at[i], kv_s.at[which], kv_r.at[which], t, head
        ).start()
        return carry

    send_key = functools.partial(send_block, pair_k, send_k, recv_k, 0)
    send_value = functools.partial(send_block, pair_v, send_v, recv_v, 1)

    edges = [1 + (NCTX - 1) * s // STEPS for s in range(STEPS + 1)]
    for s in range(STEPS):
        for d in (0, 1):
            if d == 0 or s < STEPS - 1:
                land_in(s, d, land_s, land_r).wait_recv()
                nxt = s + 1
                if nxt < STEPS - d:
                    land_ring(nxt, d, land_s, land_r).start()
                w_in(s, d, wz_s, wz_r).wait_recv()
                if nxt < STEPS - d:
                    w_ring(nxt, d, wz_s, wz_r).start()
        lax.fori_loop(edges[s], edges[s + 1], send_key, 0)

    def y_copy(buf, row, half, send, recv, j, to):
        n = buf.shape[0] // NY
        part = n // 2 if half is not None else n
        at = row * n + (half * part if half is not None else 0)
        ref = buf.at[pl.ds(at, part)]
        return remote(ref, ref, send.at[j], recv.at[j], to * NZ + z, head)

    def y_first(buf, send, recv):
        return [
            y_copy(buf, y, None, send, recv, 0, y_up),
            y_copy(buf, y, None, send, recv, 1, y_dn),
        ]

    def y_first_in(buf, send, recv):
        return [
            y_copy(buf, y_dn, None, send, recv, 0, y_up),
            y_copy(buf, y_up, None, send, recv, 1, y_dn),
        ]

    def y_second(buf, send, recv):
        return [
            y_copy(buf, y_dn, 0, send, recv, 2, y_up),
            y_copy(buf, y_up, 1, send, recv, 3, y_dn),
        ]

    def y_second_in(buf, send, recv):
        return [
            y_copy(buf, y_far, 0, send, recv, 2, y_up),
            y_copy(buf, y_far, 1, send, recv, 3, y_dn),
        ]

    for c in y_first(land_all, yl_s, yl_r):
        c.start()
    half = NZ // 2
    to_mate = remote(
        w_lane.at[pl.ds((1 - core) * half, half)],
        w_all.at[pl.ds((2 * y + core) * half, half)],
        core_sem.at[0],
        core_sem.at[1],
        ctx,
        mate,
    )
    to_mate.start()
    keep = pltpu.make_async_copy(
        w_lane.at[pl.ds(core * half, half)],
        w_all.at[pl.ds((2 * y + core) * half, half)],
        core_sem.at[2],
    )
    keep.start()
    lax.fori_loop(1, NCTX, send_value, 0)
    remote(
        w_lane.at[pl.ds(core * half, half)],
        w_all.at[pl.ds((2 * y + 1 - core) * half, half)],
        core_sem.at[0],
        core_sem.at[1],
        ctx,
        mate,
    ).wait_recv()
    keep.wait()
    for c in y_first(w_all, yw_s, yw_r):
        c.start()
    for c, f in zip(
        y_first_in(land_all, yl_s, yl_r), y_second(land_all, yl_s, yl_r)
    ):
        c.wait_recv()
        f.start()
    for c in y_second_in(land_all, yl_s, yl_r):
        c.wait_recv()

    def first_part(i, carry):
        g, h = lax.div(i, HEADS), lax.rem(i, HEADS)
        rows = pl.ds(pl.multiple_of(g * BLOCK, BLOCK), BLOCK)
        cols = pl.ds(pl.multiple_of(h * DH, DH), DH)
        qv = q[rows, cols]
        lk = land_all[:, 0:LAND, cols].reshape(NCTX * LAND, DH)
        lv = land_all[:, LAND : 2 * LAND, cols].reshape(NCTX * LAND, DH)
        s_l = lax.dot_general(qv, lk, NT, preferred_element_type=jnp.float32) * SCALE
        s_s = (
            lax.dot_general(
                qv, sk[rows, cols], NT, preferred_element_type=jnp.float32
            )
            * SCALE
        )
        causal = lax.broadcasted_iota(jnp.int32, s_s.shape, 0) >= lax.broadcasted_iota(
            jnp.int32, s_s.shape, 1
        )
        s_s = jnp.where(causal, s_s, -jnp.inf)
        m = jnp.maximum(
            jnp.max(s_l, axis=1, keepdims=True), jnp.max(s_s, axis=1, keepdims=True)
        )
        p_l, p_s = jnp.exp(s_l - m), jnp.exp(s_s - m)
        total = jnp.sum(p_l, axis=1, keepdims=True) + jnp.sum(
            p_s, axis=1, keepdims=True
        )
        acc[i] = jnp.dot(
            p_l.astype(jnp.bfloat16), lv, preferred_element_type=jnp.float32
        ) + jnp.dot(
            p_s.astype(jnp.bfloat16),
            sv[rows, cols],
            preferred_element_type=jnp.float32,
        )
        top[i] = jnp.broadcast_to(m, (BLOCK, DH))
        tot[i] = jnp.broadcast_to(total, (BLOCK, DH))
        return carry

    lax.fori_loop(0, GROUPS * HEADS, first_part, 0)

    for c, f in zip(y_first_in(w_all, yw_s, yw_r), y_second(w_all, yw_s, yw_r)):
        c.wait_recv()
        f.start()
    for c in y_second_in(w_all, yw_s, yw_r):
        c.wait_recv()

    def chosen(buf, i):
        blocks = []
        for p in range(PICKS):
            blocks.append(buf[slots[i * PICKS + p]])
        return jnp.concatenate(blocks, axis=0)

    def kv_wait(buf, sem):
        ref = buf.at[pl.ds(1, NCTX - 1)]
        pltpu.make_async_copy(ref, ref, sem).wait()

    kv_wait(recv_k, kv_r.at[0])

    def second_part(i, carry):
        g, h = lax.div(i, HEADS), lax.rem(i, HEADS)
        rows = pl.ds(pl.multiple_of(g * BLOCK, BLOCK), BLOCK)
        cols = pl.ds(pl.multiple_of(h * DH, DH), DH)
        s = (
            lax.dot_general(
                q[rows, cols],
                chosen(recv_k, i),
                NT,
                preferred_element_type=jnp.float32,
            )
            * SCALE
        )
        m_old = top[i][:, :1]
        m = jnp.maximum(m_old, jnp.max(s, axis=1, keepdims=True))
        p = jnp.exp(s - m)
        shrink = jnp.exp(m_old - m)
        prob[i] = p.astype(jnp.bfloat16)
        acc[i] = acc[i] * shrink
        total = tot[i][:, :1] * shrink + jnp.sum(p, axis=1, keepdims=True)
        tot[i] = jnp.broadcast_to(total, (BLOCK, DH))
        return carry

    lax.fori_loop(0, GROUPS * HEADS, second_part, 0)
    kv_wait(recv_v, kv_r.at[1])

    def part(h, g):
        return att.at[h, pl.ds(g * BLOCK, BLOCK)]

    def att_copy(h, g, send, recv, to):
        return remote(part(h, g), part(h, g), send, recv, ctx, to)

    started = []

    def go(c):
        c.start()
        started.append(c)

    up_lane, dn_lane, far_lane = 2 * x_up + core, 2 * x_dn + core, 2 * x_far + core
    up_mate, dn_mate = 2 * x_up + 1 - core, 2 * x_dn + 1 - core
    far_mate = 2 * x_far + 1 - core
    for g in range(GROUPS):
        for h in range(HEADS):
            i = g * HEADS + h
            total = acc[i] + jnp.dot(
                prob[i], chosen(recv_v, i), preferred_element_type=jnp.float32
            )
            att[head, g * BLOCK : (g + 1) * BLOCK, h * DH : (h + 1) * DH] = (
                total / tot[i]
            ).astype(jnp.bfloat16)
        go(att_copy(head, g, xs_s.at[0, g], xs_r.at[0, g], up_lane))
        go(att_copy(head, g, xs_s.at[1, g], xs_r.at[1, g], dn_lane))
        go(att_copy(head, g, mate_s.at[g], mate_r.at[g], mate))

    def add(h, first=False):
        prod = lax.dot_general(
            att[h],
            w_all[pl.ds(h * 8, 8)].reshape(WIDTH, WIDTH),
            NT,
            preferred_element_type=jnp.float32,
        )
        if first:
            sums[...] = prod
        else:
            sums[...] += prod

    def forward(g, d):
        lane_of = dn_lane if d == 0 else up_lane
        att_copy(lane_of, g, xs_s.at[d, g], xs_r.at[d, g], mate).wait_recv()
        if (d == 0) == (g < GROUPS // 2):
            go(
                att_copy(
                    lane_of, g, far_s.at[g], far_r.at[g], up_lane if d == 0 else dn_lane
                )
            )
        go(att_copy(lane_of, g, fwd_s.at[d, g], fwd_r.at[d, g], mate))

    for g in range(GROUPS):
        for d in (0, 1):
            forward(g, d)
        if g == 0:
            add(head, first=True)
    for g in range(GROUPS):
        att_copy(mate, g, mate_s.at[g], mate_r.at[g], mate).wait_recv()
    for g in range(GROUPS):
        att_copy(far_lane, g, far_s.at[g], far_r.at[g], mate).wait_recv()
        go(att_copy(far_lane, g, ffw_s.at[g], ffw_r.at[g], mate))
    add(mate)
    add(dn_lane)
    add(up_lane)
    for d, h in ((0, dn_mate), (1, up_mate)):
        for g in range(GROUPS):
            att_copy(h, g, fwd_s.at[d, g], fwd_r.at[d, g], mate).wait_recv()
        add(h)
    add(far_lane)
    for g in range(GROUPS):
        att_copy(far_mate, g, ffw_s.at[g], ffw_r.at[g], mate).wait_recv()
    add(far_mate)
    out[...] = sums[...].astype(jnp.bfloat16)

    for c in started:
        c.wait_send()
    kv_wait(send_k, kv_s.at[0])
    kv_wait(send_v, kv_s.at[1])
    for c in y_first(w_all, yw_s, yw_r) + y_second(w_all, yw_s, yw_r):
        c.wait_send()
    for c in y_first(land_all, yl_s, yl_r) + y_second(land_all, yl_s, yl_r):
        c.wait_send()
    to_mate.wait_send()
    for s in range(STEPS):
        for d in (0, 1):
            if s < STEPS - d:
                land_ring(s, d, land_s, land_r).wait_send()
                w_ring(s, d, wz_s, wz_r).wait_send()
    rest = pick_all.at[pl.ds(1, NCTX - 1)]
    pltpu.make_async_copy(rest, rest, pick_sem.at[0]).wait()

    @pl.when(off_diag)
    def _():
        swap.wait_send()


def local(
    queries,
    span_keys,
    span_values,
    cache_keys,
    cache_values,
    land_keys,
    land_values,
    out_weight,
    selection,
):
    picks = selection.reshape(GROUPS * HEADS * PICKS)
    pick_row = jnp.broadcast_to(jnp.pad(picks, (0, 64))[None, :], (8, 128))
    land = jnp.concatenate([land_keys, land_values], axis=0)
    bf16, f32, i32 = jnp.bfloat16, jnp.float32, jnp.int32
    vmem = pl.BlockSpec(memory_space=pltpu.VMEM)
    dma = pltpu.SemaphoreType.DMA
    pairs = GROUPS * HEADS
    return pl.pallas_call(
        kernel,
        out_shape=jax.ShapeDtypeStruct((ROWS, WIDTH), bf16),
        in_specs=[pl.BlockSpec(memory_space=pltpu.SMEM)] + [vmem] * 8,
        out_specs=vmem,
        scratch_shapes=[
            pltpu.VMEM((NCTX, 8, 128), i32),
            pltpu.VMEM((NCTX, 128), i32),
            pltpu.SMEM((NCTX, 128), i32),
            pltpu.VMEM((NCTX, 2 * LAND, WIDTH), bf16),
            pltpu.VMEM((NZ, BLOCK, WIDTH), bf16),
            pltpu.VMEM((NCTX, BLOCK, WIDTH), bf16),
            pltpu.VMEM((NCTX, BLOCK, DH), bf16),
            pltpu.VMEM((NCTX, BLOCK, DH), bf16),
            pltpu.VMEM((NCTX, BLOCK, DH), bf16),
            pltpu.VMEM((NCTX, BLOCK, DH), bf16),
            pltpu.VMEM((8, ROWS, WIDTH), bf16),
            pltpu.VMEM((pairs, BLOCK, PICKS * BLOCK), bf16),
            pltpu.VMEM((pairs, BLOCK, DH), f32),
            pltpu.VMEM((pairs, BLOCK, DH), f32),
            pltpu.VMEM((pairs, BLOCK, DH), f32),
            pltpu.VMEM((ROWS, WIDTH), f32),
            pltpu.VMEM((BLOCKS * HEADS, BLOCK, DH), bf16),
            pltpu.VMEM((BLOCKS * HEADS, BLOCK, DH), bf16),
            dma((2,)),
            dma((1,)),
            dma((2, STEPS)),
            dma((2, STEPS)),
            dma((2,)),
            dma((2, STEPS)),
            dma((2, STEPS)),
            dma((3,)),
            dma((4,)),
            dma((4,)),
            dma((4,)),
            dma((4,)),
            dma((2,)),
            dma((2,)),
            dma((GROUPS,)),
            dma((GROUPS,)),
            dma((2, GROUPS)),
            dma((2, GROUPS)),
            dma((2, GROUPS)),
            dma((2, GROUPS)),
            dma((GROUPS,)),
            dma((GROUPS,)),
            dma((GROUPS,)),
            dma((GROUPS,)),
        ],
        compiler_params=pltpu.CompilerParams(
            collective_id=0, has_side_effects=True, vmem_limit_bytes=56 << 20
        ),
        name="landmark_attention",
    )(
        slots_of(picks),
        pick_row,
        queries,
        span_keys,
        span_values,
        cache_keys,
        cache_values,
        land,
        out_weight.T,
    )


def solution(mesh):
    in_specs = (P("ctx", "head"),) * 7 + (P("head", "ctx"), P("ctx", "head", None))
    return jax.shard_map(
        local, mesh=mesh, in_specs=in_specs, out_specs=P("ctx", "head"), check_vma=False
    )
```

time: 300 us -> 195 us (0.65)
  Pallas kernels: 0 us -> 190 us
  waiting for transfers between devices: 145 us -> 0 us
  blocking collectives: 59.3 us -> 0 us
  starting transfers between devices: 30.9 us -> 0 us
  local copies, waits for them, and re-layouts: 26.3 us -> 3.06 us
  matrix products: 16 us -> 0 us
  between operations: 13.7 us -> 0.02 us
  other arithmetic: 8.17 us -> 1.94 us
    pallas_call x0 -> x1, Pallas kernels: none -> 190 us  [local(): pl.pallas_call(kernel, out_shape=jax.ShapeDtypeStruct((ROWS, WIDTH), bf16...]
    all_gather x2 -> x0, waiting for transfers between devices: 99.5 us -> none  [the longest x1 55.5 us: in_one_piece(): lax.all_gather(both, axis, axis=dim, tiled=True)]
    all_to_all x2 -> x0, blocking collectives: 48.6 us -> none  [the longest x1 39.7 us: sum_at_owner(): tiles = lax.all_to_all(cut_along(array, dim, peers), axis, 0, 0, tiled=True)]
    all_to_all x3 -> x0, waiting for transfers between devices: 45.2 us -> none  [the longest x1 35.5 us: local(): lax.all_to_all(sent_keys, CTX, split_axis=0, concat_axis=0, tiled=True)]
    all_to_all x3 -> x0, starting transfers between devices: 30.9 us -> none  [the longest x1 14.9 us: turned_blocks(): lax.all_to_all(tiles, axes[k], split_axis=k, concat_axis=k, tiled=True)]
    dot_general x7 -> x0, matrix products: 16 us -> none  [the longest x1 4.39 us: local(): jnp.einsum('hqn,nhd->hqd', weights.astype(jnp.bfloat16), value_piece, pre...]
    all_gather x1 -> x0, blocking collectives: 10.7 us -> none  [gather_in_order(): tiles = lax.all_gather(tiles, axes[k], axis=0, tiled=True)]
    reshape x12 -> x1, local copies, waits for them, and re-layouts: 7.13 us -> 0.09 us  [local(): picks = selection.reshape(GROUPS * HEADS * PICKS)]
  transfers between devices with their start and end apart: 5 -> 0, of which waited for: 4 -> 0; matrix products, arithmetic and copies ran while one was open for 15% -> 0% of each run, Pallas kernels for 0% -> 0%
where the time goes in v1:
time: 195 us
  Pallas kernels  190 us (97%)
  local copies, waits for them, and re-layouts  3.06 us (2%)
    pallas_call x1, Pallas kernels, local(): pl.pallas_call(kernel, out_shape=jax.ShapeDtypeStruct((ROWS, WIDTH), bf16...  190 us

profile of v1, /device:TPU:1, one launch (start us, length us, event | category | flops | bytes accessed | tf_op | source)
XLA Modules:
  0.0 195.1 jit_solution(11375250861760933273)
XLA Ops:
  0.0 0.0 copy-start.1
  0.0 0.0 copy-start
  0.0 0.7 copy-done.1
  0.7 0.1 reshape.4
  0.8 0.6 fusion.1.slots
  1.4 0.6 broadcast_in_dim.3.pick_row
  2.0 0.0 copy-done
  2.0 1.3 pad_maximum_fusion.land
  3.3 190.1 %landmark_attention.1 = bf16[256,512]{1,0:T(8,128)(2,1)} custom-call(s32[64]{0:T(128)} %fusion.1.slots, s32[8,128]{1,0:T(8,128)} %broadcast_in_dim.3.pick_row, bf16[256,512]{1,0:T(8,128)(2,1)} %q.1, bf16[256,512]{1,0:T(8,128)(2,1)} %sk.1, bf16[256,512]{1,0:T(8,128)(2,1)} %sv.1, bf16[1024,512]{1,0:T(8,128)(2,1)} %ck.1, bf16[1024,512]{1,0:T(8,128)(2,1)} %cv.1, ...), custom_call_target="tpu_custom_call" | custom-call | tf_op jit(solution)/shard_map/landmark_attention/pallas_call | solution.py:523
  193.5 1.7 copy.11
  (1 shorter events, 0.0 us)
Async XLA Ops:
  0.0 0.7 copy-start.1
  0.0 2.0 %copy-start = (bf16[16,512]{1,0:T(8,128)(2,1)S(1)}, bf16[16,512]{1,0:T(8,128)(2,1)}, u32[]{:S(2)}) copy-start(bf16[16,512]{1,0:T(8,128)(2,1)} %param.15) | copy-start | bytes 49156

commit v2 on v1

--- a/solution.py
+++ b/solution.py
@@ -17,6 +17,7 @@
 LAND = 16
 BLOCKS = 16
 STEPS = NZ // 2
+PER_STEP = 12
 NT = (((1,), (1,)), ((), ()))
 SCALE = 1.0 / math.sqrt(DH)
 
@@ -29,14 +30,7 @@
 
 
 def slot_of(dy, dz):
-    k = jnp.where(dz == 0, 0, jnp.where(dz <= 8, 2 * dz - 1, 2 * (NZ - dz)))
-    return 4 * k + dy
-
-
-def slots_of(picks):
-    ctx = lax.axis_index("ctx")
-    owner = picks >> 4
-    return slot_of(((ctx >> 4) - (owner >> 4)) & 3, ((ctx & 15) - (owner & 15)) & 15)
+    return NY * dz + dy
 
 
 def remote(src, dst, send, recv, ctx, head):
@@ -51,19 +45,23 @@
 
 
 def kernel(
-    slots,
+    picks,
+    q_in,
+    sk_in,
+    sv_in,
+    ck_in,
+    cv_in,
+    lk_in,
+    lv_in,
+    wt,
+    out,
     pick_row,
+    pick_all,
+    code_v,
+    code_s,
     q,
     sk,
     sv,
-    ck,
-    cv,
-    land,
-    wt,
-    out,
-    pick_all,
-    code_v,
-    code_s,
     land_all,
     w_lane,
     w_all,
@@ -81,6 +79,7 @@
     pair_v,
     pick_sem,
     code_sem,
+    in_sem,
     land_s,
     land_r,
     swap_sem,
@@ -110,8 +109,6 @@
     mate = 2 * x + 1 - core
     x_up, x_dn = lax.rem(x + 1, NX), lax.rem(x + NX - 1, NX)
     x_far = lax.rem(x + 2, NX)
-    y_up, y_dn = lax.rem(y + 1, NY), lax.rem(y + NY - 1, NY)
-    y_far = lax.rem(y + 2, NY)
     z_up = y * NZ + lax.rem(z + 1, NZ)
     z_dn = y * NZ + lax.rem(z + NZ - 1, NZ)
     swap_ctx, swap_head = x * NZ + z, 2 * y + core
@@ -132,6 +129,9 @@
     lax.fori_loop(1, NCTX, greet, 0)
     for h in (mate, 2 * x_up + core, 2 * x_dn + core):
         pl.semaphore_signal(barrier, inc=1, device_id=(ctx, h), device_id_type=MESH)
+    for dy in range(1, NY):
+        to = lax.rem(y + dy, NY) * NZ + z
+        pl.semaphore_signal(barrier, inc=1, device_id=(to, mate), device_id_type=MESH)
 
     @pl.when(off_diag)
     def _():
@@ -139,22 +139,44 @@
             barrier, inc=1, device_id=(swap_ctx, swap_head), device_id_type=MESH
         )
 
-    land_all[ctx] = land[...]
+    loads = [
+        pltpu.make_async_copy(src, dst, in_sem.at[n])
+        for n, (src, dst) in enumerate(
+            [
+                (lk_in, land_all.at[ctx, pl.ds(0, LAND)]),
+                (lv_in, land_all.at[ctx, pl.ds(LAND, LAND)]),
+            ]
+            + [
+                (src.at[:, :, pl.ds(h * DH, DH)], dst.at[pl.ds(h * BLOCKS, BLOCKS)])
+                for src, dst in ((ck_in, pair_k), (cv_in, pair_v))
+                for h in range(HEADS)
+            ]
+            + [(q_in, q), (sk_in, sk), (sv_in, sv)]
+        )
+    ]
+    for c in loads:
+        c.start()
+    own_w = pltpu.make_async_copy(wt, w_lane.at[z], swap_sem.at[2])
 
     @pl.when(x == y)
     def _():
-        w_lane[z] = wt[...]
-
-    def split(b, carry):
-        rows = pl.ds(pl.multiple_of(b * BLOCK, BLOCK), BLOCK)
-        for h in range(HEADS):
-            pair_k[b * HEADS + h] = ck[rows, h * DH : (h + 1) * DH]
-            pair_v[b * HEADS + h] = cv[rows, h * DH : (h + 1) * DH]
-        return carry
-
-    lax.fori_loop(0, BLOCKS, split, 0)
-
-    pl.semaphore_wait(barrier, NCTX - 1 + 3 + jnp.where(off_diag, 1, 0))
+        own_w.start()
+
+    lane = lax.broadcasted_iota(jnp.int32, (1, 128), 1)
+    row = jnp.zeros((1, 128), jnp.int32)
+    for j in range(GROUPS * HEADS * PICKS):
+        row = jnp.where(
+            lane == j, picks[j // (HEADS * PICKS), j // PICKS % HEADS, j % PICKS], row
+        )
+    pick_row[...] = row
+    for c in loads[:2]:
+        c.wait()
+
+    @pl.when(x == y)
+    def _():
+        own_w.wait()
+
+    pl.semaphore_wait(barrier, NCTX - 1 + 3 + NY - 1 + jnp.where(off_diag, 1, 0))
 
     def ring(buf, base, s, d, send, recv):
         slot = base + lax.rem(z + (NZ - s if d == 0 else s), NZ)
@@ -182,6 +204,30 @@
     land_in = functools.partial(ring_in, land_all, y * NZ)
     w_ring = functools.partial(ring, w_lane, 0)
     w_in = functools.partial(ring_in, w_lane, 0)
+    def spread_land(zz):
+        for dy in range(1, NY):
+            ref = land_all.at[y * NZ + zz]
+            to = lax.rem(y + dy, NY) * NZ + z
+            remote(ref, ref, yl_s.at[dy], yl_r.at[dy], to, head).start()
+
+    def spread_weights(zz):
+        src = w_lane.at[zz]
+        half_of = lax.div(zz, NZ // 2)
+        dst = w_all.at[head_row * 8 + lax.rem(zz, NZ // 2)]
+        taker = 2 * x + half_of
+        for dy in range(1, NY):
+            to = lax.rem(y + dy, NY) * NZ + z
+            remote(src, dst, yw_s.at[dy], yw_r.at[dy], to, taker).start()
+
+        @pl.when(half_of == core)
+        def _():
+            pltpu.make_async_copy(src, dst, core_sem.at[2]).start()
+
+        @pl.when(half_of != core)
+        def _():
+            remote(src, dst, core_sem.at[0], core_sem.at[1], ctx, mate).start()
+
+    head_row = 2 * y + core
     for d in (0, 1):
         land_ring(0, d, land_s, land_r).start()
     swap = remote(
@@ -214,11 +260,13 @@
 
     for d in (0, 1):
         w_ring(0, d, wz_s, wz_r).start()
+    spread_land(z)
+    spread_weights(z)
     pltpu.make_async_copy(pick_all, pick_all, pick_sem.at[1]).wait()
     asked = pick_all[:, 0, :]
     lane = lax.broadcasted_iota(jnp.int32, asked.shape, 1)
     mine = jnp.logical_and(lane < GROUPS * HEADS * PICKS, (asked >> 4) == ctx)
-    code = jnp.where(mine, (asked & 15) * HEADS + ((lane >> 2) & 3), 0)
+    code = jnp.where(mine, (asked & 15) + ((lane >> 2) & 3) * BLOCKS, 0)
     code = jnp.max(code, axis=1, keepdims=True)
     code_v[...] = jnp.broadcast_to(code, code_v.shape)
     to_scalar = pltpu.make_async_copy(code_v, code_s, code_sem.at[0])
@@ -228,11 +276,13 @@
     def block_for(cache, t):
         return cache[code_s[t, 0]]
 
+    for c in loads[2:]:
+        c.wait()
     recv_k[0] = block_for(pair_k, ctx)
     recv_v[0] = block_for(pair_v, ctx)
 
-    def send_block(cache, out_buf, in_buf, which, i, carry):
-        t = peer(i)
+    def send_block(cache, out_buf, in_buf, which, j, carry):
+        t, i = peer(j), slot_of(*offsets(j))
         out_buf[i] = block_for(cache, t)
         remote(
             out_buf.at[i], in_buf.at[i], kv_s.at[which], kv_r.at[which], t, head
@@ -242,7 +292,13 @@
     send_key = functools.partial(send_block, pair_k, send_k, recv_k, 0)
     send_value = functools.partial(send_block, pair_v, send_v, recv_v, 1)
 
-    edges = [1 + (NCTX - 1) * s // STEPS for s in range(STEPS + 1)]
+    def send_blocks(first, last):
+        cut = NCTX - 1
+        if first < cut:
+            lax.fori_loop(first + 1, min(last, cut) + 1, send_key, 0)
+        if last > cut:
+            lax.fori_loop(max(first, cut) - cut + 1, last - cut + 1, send_value, 0)
+
     for s in range(STEPS):
         for d in (0, 1):
             if d == 0 or s < STEPS - 1:
@@ -253,76 +309,19 @@
                 w_in(s, d, wz_s, wz_r).wait_recv()
                 if nxt < STEPS - d:
                     w_ring(nxt, d, wz_s, wz_r).start()
-        lax.fori_loop(edges[s], edges[s + 1], send_key, 0)
-
-    def y_copy(buf, row, half, send, recv, j, to):
-        n = buf.shape[0] // NY
-        part = n // 2 if half is not None else n
-        at = row * n + (half * part if half is not None else 0)
-        ref = buf.at[pl.ds(at, part)]
-        return remote(ref, ref, send.at[j], recv.at[j], to * NZ + z, head)
-
-    def y_first(buf, send, recv):
-        return [
-            y_copy(buf, y, None, send, recv, 0, y_up),
-            y_copy(buf, y, None, send, recv, 1, y_dn),
-        ]
-
-    def y_first_in(buf, send, recv):
-        return [
-            y_copy(buf, y_dn, None, send, recv, 0, y_up),
-            y_copy(buf, y_up, None, send, recv, 1, y_dn),
-        ]
-
-    def y_second(buf, send, recv):
-        return [
-            y_copy(buf, y_dn, 0, send, recv, 2, y_up),
-            y_copy(buf, y_up, 1, send, recv, 3, y_dn),
-        ]
-
-    def y_second_in(buf, send, recv):
-        return [
-            y_copy(buf, y_far, 0, send, recv, 2, y_up),
-            y_copy(buf, y_far, 1, send, recv, 3, y_dn),
-        ]
-
-    for c in y_first(land_all, yl_s, yl_r):
-        c.start()
-    half = NZ // 2
-    to_mate = remote(
-        w_lane.at[pl.ds((1 - core) * half, half)],
-        w_all.at[pl.ds((2 * y + core) * half, half)],
-        core_sem.at[0],
-        core_sem.at[1],
-        ctx,
-        mate,
-    )
-    to_mate.start()
-    keep = pltpu.make_async_copy(
-        w_lane.at[pl.ds(core * half, half)],
-        w_all.at[pl.ds((2 * y + core) * half, half)],
-        core_sem.at[2],
-    )
-    keep.start()
-    lax.fori_loop(1, NCTX, send_value, 0)
-    remote(
-        w_lane.at[pl.ds(core * half, half)],
-        w_all.at[pl.ds((2 * y + 1 - core) * half, half)],
-        core_sem.at[0],
-        core_sem.at[1],
-        ctx,
-        mate,
-    ).wait_recv()
-    keep.wait()
-    for c in y_first(w_all, yw_s, yw_r):
-        c.start()
-    for c, f in zip(
-        y_first_in(land_all, yl_s, yl_r), y_second(land_all, yl_s, yl_r)
-    ):
-        c.wait_recv()
-        f.start()
-    for c in y_second_in(land_all, yl_s, yl_r):
-        c.wait_recv()
+                zz = lax.rem(z + (NZ - nxt if d == 0 else nxt), NZ)
+                spread_land(zz)
+                spread_weights(zz)
+        send_blocks(PER_STEP * s, PER_STEP * (s + 1))
+
+    send_blocks(PER_STEP * STEPS, 2 * (NCTX - 1))
+
+    def row_wait(buf, sem, row, n):
+        ref = buf.at[pl.ds(row * n, n)]
+        pltpu.make_async_copy(ref, ref, sem).wait()
+
+    for dy in range(1, NY):
+        row_wait(land_all, yl_r.at[dy], lax.rem(y + NY - dy, NY), NZ)
 
     def first_part(i, carry):
         g, h = lax.div(i, HEADS), lax.rem(i, HEADS)
@@ -362,16 +361,13 @@
 
     lax.fori_loop(0, GROUPS * HEADS, first_part, 0)
 
-    for c, f in zip(y_first_in(w_all, yw_s, yw_r), y_second(w_all, yw_s, yw_r)):
-        c.wait_recv()
-        f.start()
-    for c in y_second_in(w_all, yw_s, yw_r):
-        c.wait_recv()
 
     def chosen(buf, i):
         blocks = []
         for p in range(PICKS):
-            blocks.append(buf[slots[i * PICKS + p]])
+            owner = picks[lax.div(i, HEADS), lax.rem(i, HEADS), p] >> 4
+            slot = slot_of((y - (owner >> 4)) & 3, (z - (owner & 15)) & 15)
+            blocks.append(buf[slot])
         return jnp.concatenate(blocks, axis=0)
 
     def kv_wait(buf, sem):
@@ -404,13 +400,20 @@
         return carry
 
     lax.fori_loop(0, GROUPS * HEADS, second_part, 0)
+    for dy in range(1, NY):
+        row_wait(w_all, yw_r.at[dy], lax.rem(y + NY - dy, NY), NZ)
+    row_wait(w_all, core_sem.at[1], 2 * y + 1 - core, NZ // 2)
+    row_wait(w_all, core_sem.at[2], 2 * y + core, NZ // 2)
     kv_wait(recv_v, kv_r.at[1])
 
-    def part(h, g):
-        return att.at[h, pl.ds(g * BLOCK, BLOCK)]
-
-    def att_copy(h, g, send, recv, to):
-        return remote(part(h, g), part(h, g), send, recv, ctx, to)
+    def att_copy(h, g, send, recv, to, half=None):
+        rows = (
+            pl.ds(g * BLOCK, BLOCK)
+            if half is None
+            else pl.ds(g * BLOCK + half * (BLOCK // 2), BLOCK // 2)
+        )
+        ref = att.at[h, rows]
+        return remote(ref, ref, send, recv, ctx, to)
 
     started = []
 
@@ -449,12 +452,8 @@
     def forward(g, d):
         lane_of = dn_lane if d == 0 else up_lane
         att_copy(lane_of, g, xs_s.at[d, g], xs_r.at[d, g], mate).wait_recv()
-        if (d == 0) == (g < GROUPS // 2):
-            go(
-                att_copy(
-                    lane_of, g, far_s.at[g], far_r.at[g], up_lane if d == 0 else dn_lane
-                )
-            )
+        to = up_lane if d == 0 else dn_lane
+        go(att_copy(lane_of, g, far_s.at[d, g], far_r.at[d, g], to, half=d))
         go(att_copy(lane_of, g, fwd_s.at[d, g], fwd_r.at[d, g], mate))
 
     for g in range(GROUPS):
@@ -465,7 +464,10 @@
     for g in range(GROUPS):
         att_copy(mate, g, mate_s.at[g], mate_r.at[g], mate).wait_recv()
     for g in range(GROUPS):
-        att_copy(far_lane, g, far_s.at[g], far_r.at[g], mate).wait_recv()
+        for d in (0, 1):
+            att_copy(
+                far_lane, g, far_s.at[d, g], far_r.at[d, g], mate, half=d
+            ).wait_recv()
         go(att_copy(far_lane, g, ffw_s.at[g], ffw_r.at[g], mate))
     add(mate)
     add(dn_lane)
@@ -484,11 +486,10 @@
         c.wait_send()
     kv_wait(send_k, kv_s.at[0])
     kv_wait(send_v, kv_s.at[1])
-    for c in y_first(w_all, yw_s, yw_r) + y_second(w_all, yw_s, yw_r):
-        c.wait_send()
-    for c in y_first(land_all, yl_s, yl_r) + y_second(land_all, yl_s, yl_r):
-        c.wait_send()
-    to_mate.wait_send()
+    for dy in range(1, NY):
+        row_wait(land_all, yl_s.at[dy], y, NZ)
+        row_wait(w_lane, yw_s.at[dy], 0, NZ)
+    row_wait(w_lane, core_sem.at[0], 1 - core, NZ // 2)
     for s in range(STEPS):
         for d in (0, 1):
             if s < STEPS - d:
@@ -513,9 +514,6 @@
     out_weight,
     selection,
 ):
-    picks = selection.reshape(GROUPS * HEADS * PICKS)
-    pick_row = jnp.broadcast_to(jnp.pad(picks, (0, 64))[None, :], (8, 128))
-    land = jnp.concatenate([land_keys, land_values], axis=0)
     bf16, f32, i32 = jnp.bfloat16, jnp.float32, jnp.int32
     vmem = pl.BlockSpec(memory_space=pltpu.VMEM)
     dma = pltpu.SemaphoreType.DMA
@@ -523,12 +521,17 @@
     return pl.pallas_call(
         kernel,
         out_shape=jax.ShapeDtypeStruct((ROWS, WIDTH), bf16),
-        in_specs=[pl.BlockSpec(memory_space=pltpu.SMEM)] + [vmem] * 8,
+        in_specs=[pl.BlockSpec(memory_space=pltpu.SMEM)]
+        + [pl.BlockSpec(memory_space=pl.ANY)] * 8,
         out_specs=vmem,
         scratch_shapes=[
-            pltpu.VMEM((NCTX, 8, 128), i32),
+            pltpu.VMEM((1, 128), i32),
+            pltpu.VMEM((NCTX, 1, 128), i32),
             pltpu.VMEM((NCTX, 128), i32),
             pltpu.SMEM((NCTX, 128), i32),
+            pltpu.VMEM((ROWS, WIDTH), bf16),
+            pltpu.VMEM((ROWS, WIDTH), bf16),
+            pltpu.VMEM((ROWS, WIDTH), bf16),
             pltpu.VMEM((NCTX, 2 * LAND, WIDTH), bf16),
             pltpu.VMEM((NZ, BLOCK, WIDTH), bf16),
             pltpu.VMEM((NCTX, BLOCK, WIDTH), bf16),
@@ -546,9 +549,10 @@
             pltpu.VMEM((BLOCKS * HEADS, BLOCK, DH), bf16),
             dma((2,)),
             dma((1,)),
+            dma((13,)),
             dma((2, STEPS)),
             dma((2, STEPS)),
-            dma((2,)),
+            dma((3,)),
             dma((2, STEPS)),
             dma((2, STEPS)),
             dma((3,)),
@@ -564,8 +568,8 @@
             dma((2, GROUPS)),
             dma((2, GROUPS)),
             dma((2, GROUPS)),
-            dma((GROUPS,)),
-            dma((GROUPS,)),
+            dma((2, GROUPS)),
+            dma((2, GROUPS)),
             dma((GROUPS,)),
             dma((GROUPS,)),
         ],
@@ -574,14 +578,14 @@
         ),
         name="landmark_attention",
     )(
-        slots_of(picks),
-        pick_row,
+        selection,
         queries,
         span_keys,
         span_values,
-        cache_keys,
-        cache_values,
-        land,
+        cache_keys.reshape(BLOCKS, BLOCK, WIDTH),
+        cache_values.reshape(BLOCKS, BLOCK, WIDTH),
+        land_keys,
+        land_values,
         out_weight.T,
     )
 

time: 195 us -> 157 us (0.81)
  Pallas kernels: 190 us -> 155 us
    pallas_call x1, Pallas kernels: 190 us -> 155 us  [local(): pl.pallas_call(kernel, out_shape=jax.ShapeDtypeStruct((ROWS, WIDTH), bf16...]
where the time goes in v2:
time: 157 us; the launch traced here: 156 us
  Pallas kernels  155 us (99%)
  local copies, waits for them, and re-layouts  1.67 us (1%)
    pallas_call x1, Pallas kernels, local(): pl.pallas_call(kernel, out_shape=jax.ShapeDtypeStruct((ROWS, WIDTH), bf16...  155 us

profile of v2, /device:TPU:1, one launch (start us, length us, event | category | flops | bytes accessed | tf_op | source)
XLA Modules:
  0.0 156.3 jit_solution(16228432902130257836)
XLA Ops:
  0.0 154.6 %landmark_attention.1 = bf16[256,512]{1,0:T(8,128)(2,1)} custom-call(s32[4,4,4]{2,1,0:T(4,128)} %picks.1, bf16[256,512]{1,0:T(8,128)(2,1)} %q_in.1, bf16[256,512]{1,0:T(8,128)(2,1)} %sk_in.1, bf16[256,512]{1,0:T(8,128)(2,1)} %sv_in.1, bf16[16,64,512]{2,1,0:T(8,128)(2,1)} %bitcast.3, bf16[16,64,512]{2,1,0:T(8,128)(2,1)} %bitcast.4, bf16[16,512]{1,0:T(8,128)(2,1)} %lk_in.1, ...), custom_call_target="tpu_custom_call" | custom-call | tf_op jit(solution)/shard_map/landmark_attention/pallas_call | solution.py:521
  154.6 1.7 %copy.11 = bf16[256,512]{1,0:T(8,128)(2,1)} copy(bf16[256,512]{1,0:T(8,128)(2,1)} %landmark_attention.1) | data formatting | bytes 524288

commit v3 on v2

--- a/solution.py
+++ b/solution.py
@@ -17,6 +17,8 @@
 LAND = 16
 BLOCKS = 16
 STEPS = NZ // 2
+EXTRA = 32
+LANE_ROWS = (BLOCK - EXTRA, BLOCK + EXTRA)
 PER_STEP = 12
 NT = (((1,), (1,)), ((), ()))
 SCALE = 1.0 / math.sqrt(DH)
@@ -63,7 +65,8 @@
     sk,
     sv,
     land_all,
-    w_lane,
+    w_lane0,
+    w_lane1,
     w_all,
     send_k,
     send_v,
@@ -111,8 +114,12 @@
     x_far = lax.rem(x + 2, NX)
     z_up = y * NZ + lax.rem(z + 1, NZ)
     z_dn = y * NZ + lax.rem(z + NZ - 1, NZ)
-    swap_ctx, swap_head = x * NZ + z, 2 * y + core
+    swap_ctx, swap_head = x * NZ + z, 2 * y
     off_diag = x != y
+
+    def on_lane(f):
+        for lane in (0, 1):
+            pl.when(core == lane)(functools.partial(f, lane))
 
     def peer(i):
         dy, dz = offsets(i)
@@ -126,7 +133,7 @@
         )
         return carry
 
-    lax.fori_loop(1, NCTX, greet, 0)
+    lax.fori_loop(1, NCTX, greet, 0, unroll=True)
     for h in (mate, 2 * x_up + core, 2 * x_dn + core):
         pl.semaphore_signal(barrier, inc=1, device_id=(ctx, h), device_id_type=MESH)
     for dy in range(1, NY):
@@ -135,9 +142,16 @@
 
     @pl.when(off_diag)
     def _():
-        pl.semaphore_signal(
-            barrier, inc=1, device_id=(swap_ctx, swap_head), device_id_type=MESH
-        )
+        @on_lane
+        def _(lane):
+            for c in range(lane + 1):
+                pl.semaphore_signal(
+                    barrier,
+                    inc=1,
+                    device_id=(swap_ctx, swap_head + c),
+                    device_id_type=MESH,
+                )
+
 
     loads = [
         pltpu.make_async_copy(src, dst, in_sem.at[n])
@@ -156,11 +170,33 @@
     ]
     for c in loads:
         c.start()
-    own_w = pltpu.make_async_copy(wt, w_lane.at[z], swap_sem.at[2])
+    lanes = (w_lane0, w_lane1)
+    kept = (wt.at[pl.ds(EXTRA, BLOCK - EXTRA)], wt)
+    lent = wt.at[pl.ds(0, EXTRA)]
+    place = (w_lane0.at[z], w_lane1.at[z, pl.ds(0, BLOCK)])
+    lent_place = w_lane1.at[z, pl.ds(BLOCK, EXTRA)]
+
+    def own_w(lane):
+        return pltpu.make_async_copy(kept[lane], place[lane], swap_sem.at[2])
+
+    def swap_main(lane):
+        return remote(
+            kept[lane],
+            place[lane],
+            swap_sem.at[0],
+            swap_sem.at[2],
+            swap_ctx,
+            swap_head + lane,
+        )
+
+    swap_lent = remote(
+        lent, lent_place, swap_sem.at[1], swap_sem.at[3], swap_ctx, swap_head + 1
+    )
 
     @pl.when(x == y)
     def _():
-        own_w.start()
+        on_lane(lambda lane: own_w(lane).start())
+
 
     lane = lax.broadcasted_iota(jnp.int32, (1, 128), 1)
     row = jnp.zeros((1, 128), jnp.int32)
@@ -174,9 +210,9 @@
 
     @pl.when(x == y)
     def _():
-        own_w.wait()
-
-    pl.semaphore_wait(barrier, NCTX - 1 + 3 + NY - 1 + jnp.where(off_diag, 1, 0))
+        on_lane(lambda lane: own_w(lane).wait())
+
+    pl.semaphore_wait(barrier, NCTX - 1 + 3 + NY - 1 + jnp.where(off_diag, 2 - core, 0))
 
     def ring(buf, base, s, d, send, recv):
         slot = base + lax.rem(z + (NZ - s if d == 0 else s), NZ)
@@ -202,41 +238,43 @@
 
     land_ring = functools.partial(ring, land_all, y * NZ)
     land_in = functools.partial(ring_in, land_all, y * NZ)
-    w_ring = functools.partial(ring, w_lane, 0)
-    w_in = functools.partial(ring_in, w_lane, 0)
+    w_ring = [functools.partial(ring, b, 0) for b in lanes]
+    w_in = [functools.partial(ring_in, b, 0) for b in lanes]
     def spread_land(zz):
         for dy in range(1, NY):
             ref = land_all.at[y * NZ + zz]
             to = lax.rem(y + dy, NY) * NZ + z
             remote(ref, ref, yl_s.at[dy], yl_r.at[dy], to, head).start()
 
-    def spread_weights(zz):
-        src = w_lane.at[zz]
+    def lane_rows(lane):
+        return pl.ds(0, LANE_ROWS[1]) if lane else pl.ds(LANE_ROWS[1], LANE_ROWS[0])
+
+    def spread_weights(lane, zz):
+        src = lanes[lane].at[zz]
         half_of = lax.div(zz, NZ // 2)
-        dst = w_all.at[head_row * 8 + lax.rem(zz, NZ // 2)]
+        dst = w_all.at[y, lax.rem(zz, NZ // 2), lane_rows(lane)]
         taker = 2 * x + half_of
         for dy in range(1, NY):
             to = lax.rem(y + dy, NY) * NZ + z
-            remote(src, dst, yw_s.at[dy], yw_r.at[dy], to, taker).start()
-
-        @pl.when(half_of == core)
+            remote(src, dst, yw_s.at[dy], yw_r.at[lane, dy], to, taker).start()
+
+        @pl.when(half_of == lane)
         def _():
             pltpu.make_async_copy(src, dst, core_sem.at[2]).start()
 
-        @pl.when(half_of != core)
+        @pl.when(half_of != lane)
         def _():
             remote(src, dst, core_sem.at[0], core_sem.at[1], ctx, mate).start()
 
-    head_row = 2 * y + core
     for d in (0, 1):
         land_ring(0, d, land_s, land_r).start()
-    swap = remote(
-        wt, w_lane.at[z], swap_sem.at[0], swap_sem.at[1], swap_ctx, swap_head
-    )
-
     @pl.when(off_diag)
     def _():
-        swap.start()
+        on_lane(lambda lane: swap_main(lane).start())
+
+    @pl.when(core == 0)
+    def _():
+        swap_lent.start()
 
     own_picks = pltpu.make_async_copy(pick_row, pick_all.at[ctx], pick_sem.at[1])
     own_picks.start()
@@ -252,16 +290,24 @@
         ).start()
         return carry
 
-    lax.fori_loop(1, NCTX, tell, 0)
+    lax.fori_loop(1, NCTX, tell, 0, unroll=True)
+
+    spread_land(z)
 
     @pl.when(off_diag)
     def _():
-        swap.wait_recv()
-
-    for d in (0, 1):
-        w_ring(0, d, wz_s, wz_r).start()
-    spread_land(z)
-    spread_weights(z)
+        on_lane(lambda lane: swap_main(lane).wait_recv())
+
+    @pl.when(core == 1)
+    def _():
+        swap_lent.wait_recv()
+
+    @on_lane
+    def _(lane):
+        for d in (0, 1):
+            w_ring[lane](0, d, wz_s, wz_r).start()
+        spread_weights(lane, z)
+
     pltpu.make_async_copy(pick_all, pick_all, pick_sem.at[1]).wait()
     asked = pick_all[:, 0, :]
     lane = lax.broadcasted_iota(jnp.int32, asked.shape, 1)
@@ -306,12 +352,16 @@
                 nxt = s + 1
                 if nxt < STEPS - d:
                     land_ring(nxt, d, land_s, land_r).start()
-                w_in(s, d, wz_s, wz_r).wait_recv()
-                if nxt < STEPS - d:
-                    w_ring(nxt, d, wz_s, wz_r).start()
                 zz = lax.rem(z + (NZ - nxt if d == 0 else nxt), NZ)
                 spread_land(zz)
-                spread_weights(zz)
+
+                @on_lane
+                def _(lane):
+                    w_in[lane](s, d, wz_s, wz_r).wait_recv()
+                    if nxt < STEPS - d:
+                        w_ring[lane](nxt, d, wz_s, wz_r).start()
+                    spread_weights(lane, zz)
+
         send_blocks(PER_STEP * s, PER_STEP * (s + 1))
 
     send_blocks(PER_STEP * STEPS, 2 * (NCTX - 1))
@@ -400,10 +450,21 @@
         return carry
 
     lax.fori_loop(0, GROUPS * HEADS, second_part, 0)
+    def bytes_wait(ref, sem):
+        pltpu.make_async_copy(ref, ref, sem).wait()
+
     for dy in range(1, NY):
-        row_wait(w_all, yw_r.at[dy], lax.rem(y + NY - dy, NY), NZ)
-    row_wait(w_all, core_sem.at[1], 2 * y + 1 - core, NZ // 2)
-    row_wait(w_all, core_sem.at[2], 2 * y + core, NZ // 2)
+        for lane in (0, 1):
+            bytes_wait(
+                w_all.at[lax.rem(y + NY - dy, NY), :, lane_rows(lane)],
+                yw_r.at[lane, dy],
+            )
+
+    @on_lane
+    def _(lane):
+        bytes_wait(w_all.at[y, :, lane_rows(lane)], core_sem.at[2])
+        bytes_wait(w_all.at[y, :, lane_rows(1 - lane)], core_sem.at[1])
+
     kv_wait(recv_v, kv_r.at[1])
 
     def att_copy(h, g, send, recv, to, half=None):
@@ -440,7 +501,11 @@
     def add(h, first=False):
         prod = lax.dot_general(
             att[h],
-            w_all[pl.ds(h * 8, 8)].reshape(WIDTH, WIDTH),
+            w_all[
+                lax.div(h, 2),
+                :,
+                pl.ds(pl.multiple_of((1 - lax.rem(h, 2)) * BLOCK, BLOCK), BLOCK),
+            ].reshape(WIDTH, WIDTH),
             NT,
             preferred_element_type=jnp.float32,
         )
@@ -488,19 +553,35 @@
     kv_wait(send_v, kv_s.at[1])
     for dy in range(1, NY):
         row_wait(land_all, yl_s.at[dy], y, NZ)
-        row_wait(w_lane, yw_s.at[dy], 0, NZ)
-    row_wait(w_lane, core_sem.at[0], 1 - core, NZ // 2)
+
+    @on_lane
+    def _(lane):
+        for dy in range(1, NY):
+            bytes_wait(lanes[lane], yw_s.at[dy])
+        bytes_wait(lanes[lane].at[pl.ds(0, NZ // 2)], core_sem.at[0])
+
     for s in range(STEPS):
         for d in (0, 1):
             if s < STEPS - d:
                 land_ring(s, d, land_s, land_r).wait_send()
-                w_ring(s, d, wz_s, wz_r).wait_send()
+
+    @on_lane
+    def _(lane):
+        for s in range(STEPS):
+            for d in (0, 1):
+                if s < STEPS - d:
+                    w_ring[lane](s, d, wz_s, wz_r).wait_send()
+
     rest = pick_all.at[pl.ds(1, NCTX - 1)]
     pltpu.make_async_copy(rest, rest, pick_sem.at[0]).wait()
 
     @pl.when(off_diag)
     def _():
-        swap.wait_send()
+        on_lane(lambda lane: swap_main(lane).wait_send())
+
+    @pl.when(core == 0)
+    def _():
+        swap_lent.wait_send()
 
 
 def local(
@@ -533,8 +614,9 @@
             pltpu.VMEM((ROWS, WIDTH), bf16),
             pltpu.VMEM((ROWS, WIDTH), bf16),
             pltpu.VMEM((NCTX, 2 * LAND, WIDTH), bf16),
-            pltpu.VMEM((NZ, BLOCK, WIDTH), bf16),
-            pltpu.VMEM((NCTX, BLOCK, WIDTH), bf16),
+            pltpu.VMEM((NZ, LANE_ROWS[0], WIDTH), bf16),
+            pltpu.VMEM((NZ, LANE_ROWS[1], WIDTH), bf16),
+            pltpu.VMEM((NY, NZ // 2, 2 * BLOCK, WIDTH), bf16),
             pltpu.VMEM((NCTX, BLOCK, DH), bf16),
             pltpu.VMEM((NCTX, BLOCK, DH), bf16),
             pltpu.VMEM((NCTX, BLOCK, DH), bf16),
@@ -552,14 +634,14 @@
             dma((13,)),
             dma((2, STEPS)),
             dma((2, STEPS)),
-            dma((3,)),
+            dma((4,)),
             dma((2, STEPS)),
             dma((2, STEPS)),
             dma((3,)),
             dma((4,)),
             dma((4,)),
             dma((4,)),
-            dma((4,)),
+            dma((2, 4)),
             dma((2,)),
             dma((2,)),
             dma((GROUPS,)),

time: 157 us -> 154 us (0.981)
  Pallas kernels: 155 us -> 152 us
    pallas_call x1, Pallas kernels: 155 us -> 152 us  [local(): pl.pallas_call(kernel, out_shape=jax.ShapeDtypeStruct((ROWS, WIDTH), bf16...]
where the time goes in v3:
time: 154 us; the launch traced here: 153 us
  Pallas kernels  152 us (99%)
  local copies, waits for them, and re-layouts  1.67 us (1%)
    pallas_call x1, Pallas kernels, local(): pl.pallas_call(kernel, out_shape=jax.ShapeDtypeStruct((ROWS, WIDTH), bf16...  152 us

profile of v3, /device:TPU:1, one launch (start us, length us, event | category | flops | bytes accessed | tf_op | source)
XLA Modules:
  0.0 153.3 jit_solution(3981851051697291146)
XLA Ops:
  0.0 151.7 %landmark_attention.1 = bf16[256,512]{1,0:T(8,128)(2,1)} custom-call(s32[4,4,4]{2,1,0:T(4,128)} %picks.1, bf16[256,512]{1,0:T(8,128)(2,1)} %q_in.1, bf16[256,512]{1,0:T(8,128)(2,1)} %sk_in.1, bf16[256,512]{1,0:T(8,128)(2,1)} %sv_in.1, bf16[16,64,512]{2,1,0:T(8,128)(2,1)} %bitcast.3, bf16[16,64,512]{2,1,0:T(8,128)(2,1)} %bitcast.4, bf16[16,512]{1,0:T(8,128)(2,1)} %lk_in.1, ...), custom_call_target="tpu_custom_call" | custom-call | tf_op jit(solution)/shard_map/landmark_attention/pallas_call | solution.py:602
  151.7 1.7 %copy.11 = bf16[256,512]{1,0:T(8,128)(2,1)} copy(bf16[256,512]{1,0:T(8,128)(2,1)} %landmark_attention.1) | data formatting | bytes 524288

commit v4 on v3

--- a/solution.py
+++ b/solution.py
@@ -129,7 +129,7 @@
 
     def greet(i, carry):
         pl.semaphore_signal(
-            barrier, inc=1, device_id=(peer(i), head), device_id_type=MESH
+            barrier, inc=1, device_id=(peer(NCTX - i), head), device_id_type=MESH
         )
         return carry
 
@@ -285,7 +285,7 @@
             pick_all.at[ctx],
             pick_sem.at[0],
             pick_sem.at[1],
-            peer(i),
+            peer(NCTX - i),
             head,
         ).start()
         return carry
@@ -524,8 +524,7 @@
     for g in range(GROUPS):
         for d in (0, 1):
             forward(g, d)
-        if g == 0:
-            add(head, first=True)
+    add(head, first=True)
     for g in range(GROUPS):
         att_copy(mate, g, mate_s.at[g], mate_r.at[g], mate).wait_recv()
     for g in range(GROUPS):

time: 154 us -> 153 us (level)
  no operation moved by 1% of the time
where the time goes in v4:
time: 153 us
  Pallas kernels  151 us (99%)
  local copies, waits for them, and re-layouts  1.67 us (1%)
    pallas_call x1, Pallas kernels, local(): pl.pallas_call(kernel, out_shape=jax.ShapeDtypeStruct((ROWS, WIDTH), bf16...  151 us

profile of v4, /device:TPU:1, one launch (start us, length us, event | category | flops | bytes accessed | tf_op | source)
XLA Modules:
  0.0 152.6 jit_solution(15590683371705824052)
XLA Ops:
  0.0 150.9 %landmark_attention.1 = bf16[256,512]{1,0:T(8,128)(2,1)} custom-call(s32[4,4,4]{2,1,0:T(4,128)} %picks.1, bf16[256,512]{1,0:T(8,128)(2,1)} %q_in.1, bf16[256,512]{1,0:T(8,128)(2,1)} %sk_in.1, bf16[256,512]{1,0:T(8,128)(2,1)} %sv_in.1, bf16[16,64,512]{2,1,0:T(8,128)(2,1)} %bitcast.3, bf16[16,64,512]{2,1,0:T(8,128)(2,1)} %bitcast.4, bf16[16,512]{1,0:T(8,128)(2,1)} %lk_in.1, ...), custom_call_target="tpu_custom_call" | custom-call | tf_op jit(solution)/shard_map/landmark_attention/pallas_call | solution.py:601
  150.9 1.7 %copy.11 = bf16[256,512]{1,0:T(8,128)(2,1)} copy(bf16[256,512]{1,0:T(8,128)(2,1)} %landmark_attention.1) | data formatting | bytes 524288
